TPU v7x, 32 devices: a whole 2x2x4 slice. The times are simulated.
32 devices in a mesh: ctx: 4 (over z), seq: 2 (over y), ch: 4 (over x, core).
Axes of the slice: x: 2, y: 2, z: 4, core: 2. Of those that a mesh axis runs over, the one named last changes fastest.
Arguments:
- grad_out: float32 [2, 512, 2048], P('seq', 'ch', 'ctx'), may hold values from -6 to 6
- query: float32 [2, 512, 2048], P('seq', 'ch', 'ctx'), may hold values from -6 to 6
- keys: float32 [2, 512, 2048], P('seq', 'ch', 'ctx'), may hold values from -6 to 6
- values: float32 [2, 512, 2048], P('seq', 'ch', 'ctx'), may hold values from -6 to 6
- long_filter: float32 [512, 2048], P(('ch', 'ctx')), may hold values from -6 to 6
- short_filter: float32 [512, 3], P('ch'), may hold values from -3.5 to 3.5
Outputs:
- grad_query: float32 [2, 512, 2048], P('seq', 'ch', 'ctx')
- grad_keys: float32 [2, 512, 2048], P('seq', 'ch', 'ctx')
- grad_values: float32 [2, 512, 2048], P('seq', 'ch', 'ctx')
- grad_long: float32 [512, 2048], P(('ch', 'ctx'))
All inputs are finite; a program needn't handle non-finite values.
Results may differ from a plain program's by a relative error of at most 0.0001.
Values sent between devices are 32-bit elements; how exact they have to be, the bound alone decides.
A program may use at most 64 MiB of HBM per device.

v0:
```python
import functools
import math

import jax
import jax.numpy as jnp
import numpy as np
from jax import lax
from jax.experimental import pallas as pl
from jax.experimental.pallas import tpu as pltpu
from jax.sharding import PartitionSpec as P

LANES = 128
SUBLANES = 8
MESH = pl.DeviceIdType.MESH


def plan(length):
    padded = 2 * length
    inner = LANES
    while inner * inner < 4 * padded:
        inner *= 2
    return padded, padded // inner, inner


def split_bf16(table):
    high = table.astype(jnp.bfloat16)
    low = (table - high.astype(np.float64)).astype(jnp.bfloat16)
    return high, low


def make_tables(length):
    padded, outer, inner = plan(length)
    ids = np.arange(inner)
    phase = 2.0 * math.pi / inner * (ids[:, None] * ids[None, :] % inner)
    cos, sin = np.cos(phase), np.sin(phase)
    forward = np.block([[cos, -sin], [sin, cos]])
    backward = np.block([[cos, sin], [-sin, cos]]) / padded * length ** (-0.5)
    turn = 2.0 * math.pi / padded * (np.arange(outer // 2 + 1)[:, None] * ids[None, :])
    turns = np.stack([np.cos(turn), np.sin(turn)])[:, :, None, :]
    turns = np.broadcast_to(turns, (2, outer // 2 + 1, SUBLANES, inner)).astype(np.float32)
    return (*split_bf16(forward), *split_bf16(backward), turns)


def half_fft(x):
    n = len(x)
    if n == 1:
        return [(x[0], None), (x[0], None)]
    even, odd = half_fft(x[0::2]), half_fft(x[1::2])
    bins = [None] * (n + 1)
    bins[0] = (even[0][0] + odd[0][0], None)
    bins[n] = (even[0][0] - odd[0][0], None)
    bins[n // 2] = (even[n // 2][0], -odd[n // 2][0])
    for k in range(1, n // 2):
        c, s = math.cos(math.pi * k / n), math.sin(math.pi * k / n)
        (er, ei), (orr, oi) = even[k], odd[k]
        tr = orr * c + oi * s
        ti = oi * c - orr * s
        bins[k] = (er + tr, ei + ti)
        bins[n - k] = (er - tr, ti - ei)
    return bins


def half_ifft(bins):
    n = len(bins) - 1
    if n == 1:
        return [bins[0][0] + bins[1][0]]
    even, odd = [None] * (n // 2 + 1), [None] * (n // 2 + 1)
    even[0] = (bins[0][0] + bins[n][0], None)
    odd[0] = (bins[0][0] - bins[n][0], None)
    even[n // 2] = (2.0 * bins[n // 2][0], None)
    odd[n // 2] = (-2.0 * bins[n // 2][1], None)
    for k in range(1, n // 2):
        c, s = math.cos(math.pi * k / n), math.sin(math.pi * k / n)
        (ar, ai), (br, bi) = bins[k], bins[n - k]
        even[k] = (ar + br, ai - bi)
        dr, di = ar - br, ai + bi
        odd[k] = (dr * c - di * s, dr * s + di * c)
    out = [None] * n
    out[0::2] = half_ifft(even)
    out[1::2] = half_ifft(odd)
    return out


def kernel(
    ctx,
    seqs,
    go_ref,
    q_ref,
    k_ref,
    v_ref,
    lf_ref,
    sf_ref,
    fh_ref,
    fl_ref,
    bh_ref,
    bl_ref,
    turn_ref,
    gq_ref,
    gk_ref,
    gv_ref,
    gl_ref,
    d_src,
    g_src,
    sk_ref,
    gs_ref,
    d_own,
    g_own,
    gg_src,
    cv_src,
    gg_back,
    cv_back,
    cross,
    cross_in,
    spec_h,
    spec_d,
    spec_g,
    work,
    halo,
    send_sems,
    recv_sems,
    cross_send,
    cross_recv,
    halo_send,
    halo_recv,
):
    me = lax.axis_index("ctx")
    my_seq = lax.axis_index("seq")
    chans, tok = k_ref.shape
    own = chans // ctx
    taps = sf_ref.shape[1]
    length = tok * ctx
    _, outer, inner = plan(length)
    bins = outer // 2 + 1
    chunk = work.shape[1]
    chunks = own // chunk
    per_tok = tok // inner

    def peer(off):
        return lax.rem(me + off, ctx)

    barrier = pltpu.get_barrier_semaphore()
    for off in range(1, ctx):
        pl.semaphore_signal(barrier, inc=1, device_id={"ctx": peer(off)}, device_id_type=MESH)
    for off in range(1, seqs):
        pl.semaphore_signal(
            barrier,
            inc=1,
            device_id={"seq": lax.rem(my_seq + off, seqs)},
            device_id_type=MESH,
        )
    d_src[...] = go_ref[...] * q_ref[...]
    halo[0] = k_ref[:, tok - LANES :].T[LANES - SUBLANES :, :]
    pl.semaphore_wait(barrier, ctx - 1 + seqs - 1)

    def halo_copy(which, off):
        return pltpu.make_async_remote_copy(
            src_ref=halo.at[2 * which],
            dst_ref=halo.at[2 * which + 1],
            send_sem=halo_send.at[which],
            recv_sem=halo_recv.at[which],
            device_id={"ctx": peer(off)},
            device_id_type=MESH,
        )

    def block(start, size):
        return pl.ds(pl.multiple_of(start, SUBLANES), size)

    def out_copy(kind, src, dst, off, c):
        return pltpu.make_async_remote_copy(
            src_ref=src.at[block(peer(off) * own + c * chunk, chunk)],
            dst_ref=dst.at[me, pl.ds(c * chunk, chunk)],
            send_sem=send_sems.at[kind, off, c],
            recv_sem=recv_sems.at[kind, off, c],
            device_id={"ctx": peer(off)},
            device_id_type=MESH,
        )

    def back_copy(kind, src, dst, off, c):
        return pltpu.make_async_remote_copy(
            src_ref=src.at[peer(off), pl.ds(c * chunk, chunk)],
            dst_ref=dst.at[block(me * own + c * chunk, chunk)],
            send_sem=send_sems.at[kind, off, c],
            recv_sem=recv_sems.at[kind, off, c],
            device_id={"ctx": peer(off)},
            device_id_type=MESH,
        )

    def cross_copy(off, c):
        return pltpu.make_async_remote_copy(
            src_ref=cross.at[pl.ds(0, ctx), pl.ds(c * chunk, chunk)],
            dst_ref=cross_in.at[off - 1, pl.ds(0, ctx), pl.ds(c * chunk, chunk)],
            send_sem=cross_send.at[off, c],
            recv_sem=cross_recv.at[off, c],
            device_id={"seq": lax.rem(my_seq + off, seqs)},
            device_id_type=MESH,
        )

    started = []

    def start(copy):
        copy.start()
        started.append(copy)
        return copy

    key_halo = start(halo_copy(0, 1))
    d_copies = {}
    for c in range(chunks):
        for off in range(ctx - 1, 0, -1):
            d_copies[off, c] = start(out_copy(0, d_src, d_own, off, c))
    d_own[me] = d_src[block(me * own, own)]

    key_halo.wait_recv()
    before = jnp.concatenate([halo[1]] * (LANES // SUBLANES), axis=0).T
    before = jnp.where(me > 0, before, 0.0)
    for z in range(ctx):
        rows = slice(z * own, (z + 1) * own)
        window = jnp.concatenate([before[rows], k_ref[rows, :]], axis=1)
        total = k_ref[rows, :] * sf_ref[rows, 0:1]
        for j in range(1, taps):
            total = total + pltpu.roll(window, j, 1)[:, LANES:] * sf_ref[rows, j : j + 1]
        sk_ref[rows, :] = total
        g_src[rows, :] = total * v_ref[rows, :]
    g_copies = {}
    for c in range(chunks):
        for off in range(ctx - 1, 0, -1):
            g_copies[off, c] = start(out_copy(1, g_src, g_own, off, c))
    g_own[me] = g_src[block(me * own, own)]

    def multiply(high_ref, low_ref):
        x = work[...].reshape(bins * chunk, 2 * inner)
        high = x.astype(jnp.bfloat16)
        low = (x - high.astype(jnp.float32)).astype(jnp.bfloat16)
        dot = functools.partial(jnp.dot, preferred_element_type=jnp.float32)
        y = dot(high, high_ref[...]) + dot(low, high_ref[...]) + dot(high, low_ref[...])
        return y.reshape(bins, chunk, 2 * inner)

    def transform(load, c, spec):
        def rows_step(i, carry):
            base = c * chunk + i * SUBLANES
            for lane in range(0, inner, LANES):
                x = [load(t, base, lane) for t in range(outer // 2)]
                for k, (re, im) in enumerate(half_fft(x)):
                    if k == 0:
                        re, im = re, jnp.zeros_like(re)
                    else:
                        cos = turn_ref[0, k, :, lane : lane + LANES]
                        sin = turn_ref[1, k, :, lane : lane + LANES]
                        if im is None:
                            re, im = re * cos, -re * sin
                        else:
                            re, im = re * cos + im * sin, im * cos - re * sin
                    at = block(i * SUBLANES, SUBLANES)
                    work[k, at, lane : lane + LANES] = re
                    work[k, at, inner + lane : inner + lane + LANES] = im
            return carry

        lax.fori_loop(0, chunk // SUBLANES, rows_step, 0)
        spec[:, c * chunk : (c + 1) * chunk, :] = multiply(fh_ref, fl_ref)

    def load_from(ref):
        def load(t, base, lane):
            at = (t % per_tok) * inner + lane
            return ref[t // per_tok, block(base, SUBLANES), at : at + LANES]

        return load

    def load_filter(t, base, lane):
        at = t * inner + lane
        return lf_ref[block(base, SUBLANES), at : at + LANES]

    def product(a, b, c, conjugate):
        rows = slice(c * chunk, (c + 1) * chunk)

        def step(k, carry):
            ar, ai = a[k, rows, :inner], a[k, rows, inner:]
            br, bi = b[k, rows, :inner], b[k, rows, inner:]
            if conjugate:
                work[k, :, :inner] = ar * br + ai * bi
                work[k, :, inner:] = ai * br - ar * bi
            else:
                work[k, :, :inner] = ar * br - ai * bi
                work[k, :, inner:] = ar * bi + ai * br
            return carry

        lax.fori_loop(0, bins, step, 0)

    def inverse(c, dst):
        work[...] = multiply(bh_ref, bl_ref)

        def rows_step(i, carry):
            at = block(i * SUBLANES, SUBLANES)
            for lane in range(0, inner, LANES):
                z = []
                for k in range(bins):
                    re = work[k, at, lane : lane + LANES]
                    if k == 0:
                        z.append((re, None))
                        continue
                    im = work[k, at, inner + lane : inner + lane + LANES]
                    cos = turn_ref[0, k, :, lane : lane + LANES]
                    sin = turn_ref[1, k, :, lane : lane + LANES]
                    z.append((re * cos - im * sin, re * sin + im * cos))
                for t, x in enumerate(half_ifft(z)):
                    col = (t % per_tok) * inner + lane
                    dst[t // per_tok, block(c * chunk + i * SUBLANES, SUBLANES), col : col + LANES] = x
            return carry

        lax.fori_loop(0, chunk // SUBLANES, rows_step, 0)

    def keep_own(c, src, dst):
        dst[block(me * own + c * chunk, chunk)] = src[me, pl.ds(c * chunk, chunk)]

    for c in range(chunks):
        transform(load_filter, c, spec_h)

    gg_copies, cv_copies, cross_copies = {}, {}, {}
    for c in range(chunks):
        for off in range(1, ctx):
            d_copies[off, c].wait_recv()
        transform(load_from(d_own), c, spec_d)
        product(spec_d, spec_h, c, True)
        inverse(c, gg_src)
        for off in range(ctx - 1, 0, -1):
            gg_copies[off, c] = start(back_copy(2, gg_src, gg_back, off, c))
        keep_own(c, gg_src, gg_back)
    for c in range(chunks):
        for off in range(1, ctx):
            g_copies[off, c].wait_recv()
        transform(load_from(g_own), c, spec_g)
        product(spec_g, spec_h, c, False)
        inverse(c, cv_src)
        for off in range(ctx - 1, 0, -1):
            cv_copies[off, c] = start(back_copy(3, cv_src, cv_back, off, c))
        product(spec_d, spec_g, c, True)
        inverse(c, cross)
        for off in range(1, seqs):
            cross_copies[off, c] = start(cross_copy(off, c))
        keep_own(c, cv_src, cv_back)

    for copy in gg_copies.values():
        copy.wait_recv()
    grad_gated = gg_back[...]
    gs_ref[...] = grad_gated * v_ref[...]
    halo[2] = gs_ref[:, :LANES].T[:SUBLANES, :]
    head_halo = start(halo_copy(1, ctx - 1))
    gv_ref[...] = gg_back[...] * sk_ref[...]
    head_halo.wait_recv()
    after = jnp.concatenate([halo[3]] * (LANES // SUBLANES), axis=0).T
    after = jnp.where(me < ctx - 1, after, 0.0)
    for z in range(ctx):
        rows = slice(z * own, (z + 1) * own)
        window = jnp.concatenate([gs_ref[rows, :], after[rows]], axis=1)
        total = gs_ref[rows, :] * sf_ref[rows, 0:1]
        for j in range(1, taps):
            total = total + pltpu.roll(window, tok + LANES - j, 1)[:, :tok] * sf_ref[rows, j : j + 1]
        gk_ref[rows, :] = total

    for (off, c), copy in cv_copies.items():
        copy.wait_recv()
    gq_ref[...] = go_ref[...] * cv_back[...]

    for copy in cross_copies.values():
        copy.wait_recv()
    for z in range(ctx):
        total = cross[z]
        for off in range(1, seqs):
            total = total + cross_in[off - 1, z]
        gl_ref[:, z * tok : (z + 1) * tok] = total
    for copy in started:
        copy.wait_send()


def shards(ctx, seqs, grad_out, query, keys, values, long_filter, short_filter):
    chans, tok = keys.shape[1:]
    own = chans // ctx
    length = tok * ctx
    _, outer, inner = plan(length)
    bins = outer // 2 + 1
    chunk = math.gcd(own, 16)
    chunks = own // chunk
    tables = make_tables(length)
    f32 = jnp.float32
    tokens = jax.ShapeDtypeStruct((chans, tok), f32)
    vmem = pl.BlockSpec(memory_space=pltpu.VMEM)
    position = pltpu.VMEM((chans, tok), f32)
    channel = pltpu.VMEM((ctx, own, tok), f32)
    spectrum = pltpu.VMEM((bins, own, 2 * inner), f32)
    dma = pltpu.SemaphoreType.DMA
    operands = [x.reshape(chans, tok) for x in (grad_out, query, keys, values)]
    operands += [long_filter, short_filter, *(jnp.asarray(t) for t in tables)]
    outs = pl.pallas_call(
        functools.partial(kernel, ctx, seqs),
        out_shape=(tokens, tokens, tokens, jax.ShapeDtypeStruct((own, length), f32)),
        in_specs=[vmem] * len(operands),
        out_specs=(vmem,) * 4,
        scratch_shapes=[
            position,
            position,
            position,
            position,
            channel,
            channel,
            channel,
            channel,
            position,
            position,
            channel,
            pltpu.VMEM((max(seqs - 1, 1), ctx, own, tok), f32),
            spectrum,
            spectrum,
            spectrum,
            pltpu.VMEM((bins, chunk, 2 * inner), f32),
            pltpu.VMEM((4, SUBLANES, chans), f32),
            dma((4, ctx, chunks)),
            dma((4, ctx, chunks)),
            dma((seqs, chunks)),
            dma((seqs, chunks)),
            dma((2,)),
            dma((2,)),
        ],
        compiler_params=pltpu.CompilerParams(
            collective_id=0, has_side_effects=True, vmem_limit_bytes=48 * 1024 * 1024
        ),
    )(*operands)
    gq, gk, gv, gl = outs
    return (gq[None], gk[None], gv[None], gl)


def solution(mesh):
    tokens = P("seq", "ch", "ctx")
    return jax.shard_map(
        functools.partial(shards, mesh.shape["ctx"], mesh.shape["seq"]),
        mesh=mesh,
        in_specs=(tokens, tokens, tokens, tokens, P(("ch", "ctx"), None), P("ch", None)),
        out_specs=(tokens, tokens, tokens, P(("ch", "ctx"), None)),
        check_vma=False,
    )
```

profile of v0, /device:TPU:0, one launch (start us, length us, event | category | flops | bytes accessed | tf_op | source)
XLA Modules:
  0.0 42.9 jit_solution(4473231895486129669)
XLA Ops:
  0.6 0.0 copy-start.10
  0.6 0.7 %copy-done.10 = f32[128,3]{0,1:T(4,128)S(1)} copy-done((f32[128,3]{0,1:T(4,128)S(1)}, f32[128,3]{0,1:T(4,128)}, u32[]{:S(2)}) %copy-start.10) | copy-done | bytes 1560
  1.3 0.1 copy.15.sf_ref
  1.4 0.0 copy-start
  1.4 0.9 %copy-done = f32[1,128,512]{2,1,0:T(8,128)S(1)} copy-done((f32[1,128,512]{2,1,0:T(8,128)S(1)}, f32[1,128,512]{2,1,0:T(8,128)}, u32[]{:S(2)}) %copy-start) | copy-done | bytes 262168
  2.4 0.0 copy-start.1
  2.4 0.9 %copy-done.1 = f32[1,128,512]{2,1,0:T(8,128)S(1)} copy-done((f32[1,128,512]{2,1,0:T(8,128)S(1)}, f32[1,128,512]{2,1,0:T(8,128)}, u32[]{:S(2)}) %copy-start.1) | copy-done | bytes 262168
  3.3 0.0 copy-start.2
  3.3 0.9 %copy-done.2 = f32[1,128,512]{2,1,0:T(8,128)S(1)} copy-done((f32[1,128,512]{2,1,0:T(8,128)S(1)}, f32[1,128,512]{2,1,0:T(8,128)}, u32[]{:S(2)}) %copy-start.2) | copy-done | bytes 262168
  4.3 0.0 copy-start.3
  4.3 0.9 %copy-done.3 = f32[1,128,512]{2,1,0:T(8,128)S(1)} copy-done((f32[1,128,512]{2,1,0:T(8,128)S(1)}, f32[1,128,512]{2,1,0:T(8,128)}, u32[]{:S(2)}) %copy-start.3) | copy-done | bytes 262168
  5.2 0.0 copy-start.4
  5.2 0.9 %copy-done.4 = f32[32,2048]{1,0:T(8,128)S(1)} copy-done((f32[32,2048]{1,0:T(8,128)S(1)}, f32[32,2048]{1,0:T(8,128)}, u32[]{:S(2)}) %copy-start.4) | copy-done | bytes 262168
  6.2 0.0 copy-start.5
  6.2 0.9 %copy-done.5 = f32[2,17,8,128]{3,2,1,0:T(8,128)S(1)} copy-done((f32[2,17,8,128]{3,2,1,0:T(8,128)S(1)}, f32[2,17,8,128]{3,2,1,0:T(8,128)}, u32[]{:S(2)}) %copy-start.5) | copy-done | bytes 139288
  7.1 0.9 %copy-done.6 = bf16[256,256]{1,0:T(8,128)(2,1)S(1)} copy-done((bf16[256,256]{1,0:T(8,128)(2,1)S(1)}, bf16[256,256]{1,0:T(8,128)(2,1)}, u32[]{:S(2)}) %copy-start.6) | copy-done | bytes 131096
  8.0 0.9 %copy-done.7 = bf16[256,256]{1,0:T(8,128)(2,1)S(1)} copy-done((bf16[256,256]{1,0:T(8,128)(2,1)S(1)}, bf16[256,256]{1,0:T(8,128)(2,1)}, u32[]{:S(2)}) %copy-start.7) | copy-done | bytes 131096
  8.9 0.9 %copy-done.8 = bf16[256,256]{1,0:T(8,128)(2,1)S(1)} copy-done((bf16[256,256]{1,0:T(8,128)(2,1)S(1)}, bf16[256,256]{1,0:T(8,128)(2,1)}, u32[]{:S(2)}) %copy-start.8) | copy-done | bytes 131096
  9.8 0.9 %copy-done.9 = bf16[256,256]{1,0:T(8,128)(2,1)S(1)} copy-done((bf16[256,256]{1,0:T(8,128)(2,1)S(1)}, bf16[256,256]{1,0:T(8,128)(2,1)}, u32[]{:S(2)}) %copy-start.9) | copy-done | bytes 131096
  10.7 29.4 %shard_map.138 = (f32[128,512]{1,0:T(8,128)S(1)}, f32[128,512]{1,0:T(8,128)S(1)}, f32[128,512]{1,0:T(8,128)S(1)}, f32[32,2048]{1,0:T(8,128)S(1)}) custom-call(f32[128,512]{1,0:T(8,128)S(1)} %bitcast.10, f32[128,512]{1,0:T(8,128)S(1)} %bitcast.11, f32[128,512]{1,0:T(8,128)S(1)} %bitcast.12, f32[128,512]{1,0:T(8,128)S(1)} %bitcast.13, ...), custom_call_target="tpu_custom_call" | custom-call | tf_op jit(solution)/shard_map/pallas_call | solution.py:391
  40.1 0.7 %copy.20 = f32[1,128,512]{2,1,0:T(8,128)} copy(f32[1,128,512]{2,1,0:T(8,128)S(1)} %bitcast.9) | data formatting | bytes 524288
  40.8 0.7 %copy.21 = f32[1,128,512]{2,1,0:T(8,128)} copy(f32[1,128,512]{2,1,0:T(8,128)S(1)} %bitcast.8) | data formatting | bytes 524288
  41.5 0.7 %copy.22 = f32[1,128,512]{2,1,0:T(8,128)} copy(f32[1,128,512]{2,1,0:T(8,128)S(1)} %bitcast.7) | data formatting | bytes 524288
  42.2 0.7 %copy.23 = f32[32,2048]{1,0:T(8,128)} copy(f32[32,2048]{1,0:T(8,128)S(1)} %get-tuple-element.19) | data formatting | bytes 524288
  (4 shorter events, 0.0 us)
Async XLA Ops:
  0.6 0.7 %copy-start.10 = (f32[128,3]{0,1:T(4,128)S(1)}, f32[128,3]{0,1:T(4,128)}, u32[]{:S(2)}) copy-start(f32[128,3]{0,1:T(4,128)} %param.16) | copy-start | bytes 4612
  1.4 0.9 %copy-start = (f32[1,128,512]{2,1,0:T(8,128)S(1)}, f32[1,128,512]{2,1,0:T(8,128)}, u32[]{:S(2)}) copy-start(f32[1,128,512]{2,1,0:T(8,128)} %param.11) | copy-start | bytes 786436
  2.4 0.9 %copy-start.1 = (f32[1,128,512]{2,1,0:T(8,128)S(1)}, f32[1,128,512]{2,1,0:T(8,128)}, u32[]{:S(2)}) copy-start(f32[1,128,512]{2,1,0:T(8,128)} %param.12) | copy-start | bytes 786436
  3.3 0.9 %copy-start.2 = (f32[1,128,512]{2,1,0:T(8,128)S(1)}, f32[1,128,512]{2,1,0:T(8,128)}, u32[]{:S(2)}) copy-start(f32[1,128,512]{2,1,0:T(8,128)} %param.13) | copy-start | bytes 786436
  4.3 0.9 %copy-start.3 = (f32[1,128,512]{2,1,0:T(8,128)S(1)}, f32[1,128,512]{2,1,0:T(8,128)}, u32[]{:S(2)}) copy-start(f32[1,128,512]{2,1,0:T(8,128)} %param.14) | copy-start | bytes 786436
  5.2 0.9 %copy-start.4 = (f32[32,2048]{1,0:T(8,128)S(1)}, f32[32,2048]{1,0:T(8,128)}, u32[]{:S(2)}) copy-start(f32[32,2048]{1,0:T(8,128)} %lf_ref.1) | copy-start | bytes 786436
  6.2 0.9 %copy-start.5 = (f32[2,17,8,128]{3,2,1,0:T(8,128)S(1)}, f32[2,17,8,128]{3,2,1,0:T(8,128)}, u32[]{:S(2)}) copy-start(f32[2,17,8,128]{3,2,1,0:T(8,128)} %constant.14.clone.turn_ref) | copy-start | bytes 417796
  7.1 0.9 %copy-start.6 = (bf16[256,256]{1,0:T(8,128)(2,1)S(1)}, bf16[256,256]{1,0:T(8,128)(2,1)}, u32[]{:S(2)}) copy-start(bf16[256,256]{1,0:T(8,128)(2,1)} %constant.13.clone.bl_ref) | copy-start | bytes 393220
  8.0 0.9 %copy-start.7 = (bf16[256,256]{1,0:T(8,128)(2,1)S(1)}, bf16[256,256]{1,0:T(8,128)(2,1)}, u32[]{:S(2)}) copy-start(bf16[256,256]{1,0:T(8,128)(2,1)} %constant.12.clone.bh_ref) | copy-start | bytes 393220
  8.9 0.9 %copy-start.8 = (bf16[256,256]{1,0:T(8,128)(2,1)S(1)}, bf16[256,256]{1,0:T(8,128)(2,1)}, u32[]{:S(2)}) copy-start(bf16[256,256]{1,0:T(8,128)(2,1)} %constant.11.clone.fl_ref) | copy-start | bytes 393220
  9.8 0.9 %copy-start.9 = (bf16[256,256]{1,0:T(8,128)(2,1)S(1)}, bf16[256,256]{1,0:T(8,128)(2,1)}, u32[]{:S(2)}) copy-start(bf16[256,256]{1,0:T(8,128)(2,1)} %constant.10.clone.fh_ref) | copy-start | bytes 393220
where the time goes:
time: 43.3 us; the launch traced here: 42.9 us
  Pallas kernels  29.4 us (68%)
  local copies, waits for them, and re-layouts  12.9 us (30%)
  between operations  0.66 us (2%)
    pallas_call x1, Pallas kernels, shards(): pl.pallas_call(functools.partial(kernel, ctx, seqs), out_shape=(tokens, t...  29.4 us
    unnamed x27, local copies, waits for them, and re-layouts  12.9 us

commit v1 on v0

--- a/solution.py
+++ b/solution.py
@@ -10,6 +10,7 @@
 from jax.sharding import PartitionSpec as P
 
 LANES = 128
+VMEM_BYTES = 62 * 1024 * 1024
 SUBLANES = 8
 MESH = pl.DeviceIdType.MESH
 
@@ -20,12 +21,6 @@
     while inner * inner < 4 * padded:
         inner *= 2
     return padded, padded // inner, inner
-
-
-def split_bf16(table):
-    high = table.astype(jnp.bfloat16)
-    low = (table - high.astype(np.float64)).astype(jnp.bfloat16)
-    return high, low
 
 
 def make_tables(length):
@@ -38,7 +33,8 @@
     turn = 2.0 * math.pi / padded * (np.arange(outer // 2 + 1)[:, None] * ids[None, :])
     turns = np.stack([np.cos(turn), np.sin(turn)])[:, :, None, :]
     turns = np.broadcast_to(turns, (2, outer // 2 + 1, SUBLANES, inner)).astype(np.float32)
-    return (*split_bf16(forward), *split_bf16(backward), turns)
+    products = np.concatenate([forward, backward]).astype(np.float32)
+    return products, turns
 
 
 def half_fft(x):
@@ -84,21 +80,29 @@
 def kernel(
     ctx,
     seqs,
+    go_hbm,
+    q_hbm,
+    k_hbm,
+    v_hbm,
+    lf_hbm,
+    sf_hbm,
+    table_hbm,
+    turn_hbm,
+    gq_ref,
+    gk_ref,
+    gv_ref,
+    gl_ref,
     go_ref,
     q_ref,
     k_ref,
     v_ref,
     lf_ref,
     sf_ref,
-    fh_ref,
-    fl_ref,
-    bh_ref,
-    bl_ref,
+    table_ref,
     turn_ref,
-    gq_ref,
-    gk_ref,
-    gv_ref,
-    gl_ref,
+    load_sems,
+    table_split,
+    taps_ref,
     d_src,
     g_src,
     sk_ref,
@@ -127,7 +131,7 @@
     my_seq = lax.axis_index("seq")
     chans, tok = k_ref.shape
     own = chans // ctx
-    taps = sf_ref.shape[1]
+    taps = sf_ref.shape[0]
     length = tok * ctx
     _, outer, inner = plan(length)
     bins = outer // 2 + 1
@@ -148,7 +152,26 @@
             device_id={"seq": lax.rem(my_seq + off, seqs)},
             device_id_type=MESH,
         )
+    pairs = (
+        (go_hbm, go_ref),
+        (q_hbm, q_ref),
+        (k_hbm, k_ref),
+        (sf_hbm, sf_ref),
+        (v_hbm, v_ref),
+        (lf_hbm, lf_ref),
+        (turn_hbm, turn_ref),
+        (table_hbm, table_ref),
+    )
+    loads = [
+        pltpu.make_async_copy(src, dst, load_sems.at[i]) for i, (src, dst) in enumerate(pairs)
+    ]
+    for load in loads:
+        load.start()
+    go_load, q_load, k_load, sf_load, v_load, lf_load, turn_load, table_load = loads
+    go_load.wait()
+    q_load.wait()
     d_src[...] = go_ref[...] * q_ref[...]
+    k_load.wait()
     halo[0] = k_ref[:, tok - LANES :].T[LANES - SUBLANES :, :]
     pl.semaphore_wait(barrier, ctx - 1 + seqs - 1)
 
@@ -209,15 +232,23 @@
             d_copies[off, c] = start(out_copy(0, d_src, d_own, off, c))
     d_own[me] = d_src[block(me * own, own)]
 
+    sf_load.wait()
+    for j in range(taps):
+        taps_ref[j] = jnp.broadcast_to(sf_ref[j : j + 1, :], (LANES, chans)).T
+
+    def tap(j, rows):
+        return jnp.concatenate([taps_ref[j, rows, :]] * (tok // LANES), axis=1)
+
+    v_load.wait()
     key_halo.wait_recv()
     before = jnp.concatenate([halo[1]] * (LANES // SUBLANES), axis=0).T
     before = jnp.where(me > 0, before, 0.0)
     for z in range(ctx):
         rows = slice(z * own, (z + 1) * own)
         window = jnp.concatenate([before[rows], k_ref[rows, :]], axis=1)
-        total = k_ref[rows, :] * sf_ref[rows, 0:1]
+        total = k_ref[rows, :] * tap(0, rows)
         for j in range(1, taps):
-            total = total + pltpu.roll(window, j, 1)[:, LANES:] * sf_ref[rows, j : j + 1]
+            total = total + pltpu.roll(window, j, 1)[:, LANES:] * tap(j, rows)
         sk_ref[rows, :] = total
         g_src[rows, :] = total * v_ref[rows, :]
     g_copies = {}
@@ -226,12 +257,18 @@
             g_copies[off, c] = start(out_copy(1, g_src, g_own, off, c))
     g_own[me] = g_src[block(me * own, own)]
 
-    def multiply(high_ref, low_ref):
+    def split(x):
+        high = x.astype(jnp.bfloat16)
+        return high, (x - high.astype(jnp.float32)).astype(jnp.bfloat16)
+
+    def table(i):
+        return table_split[i]
+
+    def multiply(first):
         x = work[...].reshape(bins * chunk, 2 * inner)
-        high = x.astype(jnp.bfloat16)
-        low = (x - high.astype(jnp.float32)).astype(jnp.bfloat16)
+        high, low = split(x)
         dot = functools.partial(jnp.dot, preferred_element_type=jnp.float32)
-        y = dot(high, high_ref[...]) + dot(low, high_ref[...]) + dot(high, low_ref[...])
+        y = dot(high, table(first)) + dot(low, table(first)) + dot(high, table(first + 1))
         return y.reshape(bins, chunk, 2 * inner)
 
     def transform(load, c, spec):
@@ -255,7 +292,7 @@
             return carry
 
         lax.fori_loop(0, chunk // SUBLANES, rows_step, 0)
-        spec[:, c * chunk : (c + 1) * chunk, :] = multiply(fh_ref, fl_ref)
+        spec[:, c * chunk : (c + 1) * chunk, :] = multiply(0)
 
     def load_from(ref):
         def load(t, base, lane):
@@ -285,7 +322,7 @@
         lax.fori_loop(0, bins, step, 0)
 
     def inverse(c, dst):
-        work[...] = multiply(bh_ref, bl_ref)
+        work[...] = multiply(2)
 
         def rows_step(i, carry):
             at = block(i * SUBLANES, SUBLANES)
@@ -310,6 +347,12 @@
     def keep_own(c, src, dst):
         dst[block(me * own + c * chunk, chunk)] = src[me, pl.ds(c * chunk, chunk)]
 
+    lf_load.wait()
+    turn_load.wait()
+    table_load.wait()
+    for i in range(2):
+        whole = table_ref[i * 2 * inner : (i + 1) * 2 * inner, :]
+        table_split[2 * i], table_split[2 * i + 1] = split(whole)
     for c in range(chunks):
         transform(load_filter, c, spec_h)
 
@@ -350,9 +393,9 @@
     for z in range(ctx):
         rows = slice(z * own, (z + 1) * own)
         window = jnp.concatenate([gs_ref[rows, :], after[rows]], axis=1)
-        total = gs_ref[rows, :] * sf_ref[rows, 0:1]
+        total = gs_ref[rows, :] * tap(0, rows)
         for j in range(1, taps):
-            total = total + pltpu.roll(window, tok + LANES - j, 1)[:, :tok] * sf_ref[rows, j : j + 1]
+            total = total + pltpu.roll(window, tok + LANES - j, 1)[:, :tok] * tap(j, rows)
         gk_ref[rows, :] = total
 
     for (off, c), copy in cv_copies.items():
@@ -368,6 +411,17 @@
         gl_ref[:, z * tok : (z + 1) * tok] = total
     for copy in started:
         copy.wait_send()
+
+
+def store(*refs):
+    count = (len(refs) - 1) // 2
+    copies = [
+        pltpu.make_async_copy(refs[i], refs[count + i], refs[-1].at[i]) for i in range(count)
+    ]
+    for copy in copies:
+        copy.start()
+    for copy in copies:
+        copy.wait()
 
 
 def shards(ctx, seqs, grad_out, query, keys, values, long_filter, short_filter):
@@ -387,13 +441,18 @@
     spectrum = pltpu.VMEM((bins, own, 2 * inner), f32)
     dma = pltpu.SemaphoreType.DMA
     operands = [x.reshape(chans, tok) for x in (grad_out, query, keys, values)]
-    operands += [long_filter, short_filter, *(jnp.asarray(t) for t in tables)]
+    operands += [long_filter, short_filter.T, *(jnp.asarray(t) for t in tables)]
+    hbm = pl.BlockSpec(memory_space=pltpu.HBM)
     outs = pl.pallas_call(
         functools.partial(kernel, ctx, seqs),
         out_shape=(tokens, tokens, tokens, jax.ShapeDtypeStruct((own, length), f32)),
-        in_specs=[vmem] * len(operands),
+        in_specs=[hbm] * len(operands),
         out_specs=(vmem,) * 4,
         scratch_shapes=[
+            *(pltpu.VMEM(operands[i].shape, operands[i].dtype) for i in range(len(operands))),
+            dma((len(operands),)),
+            pltpu.VMEM((4, 2 * inner, 2 * inner), jnp.bfloat16),
+            pltpu.VMEM((short_filter.shape[1], chans, LANES), f32),
             position,
             position,
             position,
@@ -419,10 +478,17 @@
             dma((2,)),
         ],
         compiler_params=pltpu.CompilerParams(
-            collective_id=0, has_side_effects=True, vmem_limit_bytes=48 * 1024 * 1024
+            collective_id=0, has_side_effects=True, vmem_limit_bytes=VMEM_BYTES
         ),
     )(*operands)
-    gq, gk, gv, gl = outs
+    gq, gk, gv, gl = pl.pallas_call(
+        store,
+        out_shape=tuple(jax.ShapeDtypeStruct(x.shape, f32) for x in outs),
+        in_specs=[hbm] * 4,
+        out_specs=(hbm,) * 4,
+        scratch_shapes=[dma((4,))],
+        compiler_params=pltpu.CompilerParams(vmem_limit_bytes=VMEM_BYTES),
+    )(*outs)
     return (gq[None], gk[None], gv[None], gl)
 
 

time: 43.3 us -> 64.3 us (1.48)
  Pallas kernels: 29.4 us -> 63.5 us
  local copies, waits for them, and re-layouts: 12.9 us -> 0 us
    pallas_call x0 -> x1, Pallas kernels: none -> 32.9 us  [shards(): pl.pallas_call(store, out_shape=tuple((jax.ShapeDtypeStruct(x.shape, f32)...]
    unnamed x27 -> x0, local copies, waits for them, and re-layouts: 12.9 us -> none
    pallas_call x1, Pallas kernels: 29.4 us -> 30.6 us  [shards(): pl.pallas_call(functools.partial(kernel, ctx, seqs), out_shape=(tokens, t...]
where the time goes in v1:
time: 64.3 us; the launch traced here: 64.1 us
  Pallas kernels  63.5 us (99%)
    pallas_call x1, Pallas kernels, shards(): pl.pallas_call(store, out_shape=tuple((jax.ShapeDtypeStruct(x.shape, f32)...  32.9 us
    pallas_call x1, Pallas kernels, shards(): pl.pallas_call(functools.partial(kernel, ctx, seqs), out_shape=(tokens, t...  30.6 us

profile of v1, /device:TPU:0, one launch (start us, length us, event | category | flops | bytes accessed | tf_op | source)
XLA Modules:
  0.0 64.1 jit_solution(7289589192664137365)
XLA Ops:
  0.6 30.6 %shard_map.111 = (f32[128,512]{1,0:T(8,128)}, f32[128,512]{1,0:T(8,128)}, f32[128,512]{1,0:T(8,128)}, f32[32,2048]{1,0:T(8,128)}) custom-call(f32[128,512]{1,0:T(8,128)} %bitcast.8, f32[128,512]{1,0:T(8,128)} %bitcast.9, f32[128,512]{1,0:T(8,128)} %bitcast.10, f32[128,512]{1,0:T(8,128)} %bitcast.11, f32[32,2048]{1,0:T(8,128)} %lf_hbm.1, f32[3,128]{1,0:T(4,128)} %bitcast.12, ...), custom_call_target="tpu_custom_call" | custom-call | tf_op jit(solution)/shard_map/pallas_call | solution.py:446
  31.2 32.9 %shard_map.112 = (f32[128,512]{1,0:T(8,128)}, f32[128,512]{1,0:T(8,128)}, f32[128,512]{1,0:T(8,128)}, f32[32,2048]{1,0:T(8,128)}) custom-call(f32[128,512]{1,0:T(8,128)} %get-tuple-element.12.refs_0_, f32[128,512]{1,0:T(8,128)} %get-tuple-element.13.refs_1_, f32[128,512]{1,0:T(8,128)} %get-tuple-element.14.refs_2_, f32[32,2048]{1,0:T(8,128)} %get-tuple-element.15.refs_3_), custom_call_target="tpu_custom_call" | custom-call | tf_op jit(solution)/shard_map/pallas_call | solution.py:484

commit v2 on v1

--- a/solution.py
+++ b/solution.py
@@ -88,10 +88,13 @@
     sf_hbm,
     table_hbm,
     turn_hbm,
-    gq_ref,
+    gk_hbm,
+    gv_hbm,
+    cv_back,
+    part_hbm,
+    cross_in,
     gk_ref,
     gv_ref,
-    gl_ref,
     go_ref,
     q_ref,
     k_ref,
@@ -112,9 +115,7 @@
     gg_src,
     cv_src,
     gg_back,
-    cv_back,
     cross,
-    cross_in,
     spec_h,
     spec_d,
     spec_g,
@@ -126,6 +127,8 @@
     cross_recv,
     halo_send,
     halo_recv,
+    store_sems,
+    keep_sems,
 ):
     me = lax.axis_index("ctx")
     my_seq = lax.axis_index("seq")
@@ -344,8 +347,18 @@
 
         lax.fori_loop(0, chunk // SUBLANES, rows_step, 0)
 
-    def keep_own(c, src, dst):
-        dst[block(me * own + c * chunk, chunk)] = src[me, pl.ds(c * chunk, chunk)]
+    def own_rows(c):
+        return block(me * own + c * chunk, chunk)
+
+    def chunk_rows(c):
+        return pl.ds(c * chunk, chunk)
+
+    stores = []
+
+    def store(src, dst, sem):
+        copy = pltpu.make_async_copy(src, dst, sem)
+        copy.start()
+        stores.append(copy)
 
     lf_load.wait()
     turn_load.wait()
@@ -365,7 +378,7 @@
         inverse(c, gg_src)
         for off in range(ctx - 1, 0, -1):
             gg_copies[off, c] = start(back_copy(2, gg_src, gg_back, off, c))
-        keep_own(c, gg_src, gg_back)
+        gg_back[own_rows(c)] = gg_src[me, chunk_rows(c)]
     for c in range(chunks):
         for off in range(1, ctx):
             g_copies[off, c].wait_recv()
@@ -378,7 +391,12 @@
         inverse(c, cross)
         for off in range(1, seqs):
             cross_copies[off, c] = start(cross_copy(off, c))
-        keep_own(c, cv_src, cv_back)
+        store(cv_src.at[me, chunk_rows(c)], cv_back.at[own_rows(c)], keep_sems.at[0, c])
+        store(
+            cross.at[pl.ds(0, ctx), chunk_rows(c)],
+            part_hbm.at[pl.ds(0, ctx), chunk_rows(c)],
+            keep_sems.at[1, c],
+        )
 
     for copy in gg_copies.values():
         copy.wait_recv()
@@ -387,6 +405,7 @@
     halo[2] = gs_ref[:, :LANES].T[:SUBLANES, :]
     head_halo = start(halo_copy(1, ctx - 1))
     gv_ref[...] = gg_back[...] * sk_ref[...]
+    store(gv_ref, gv_hbm, store_sems.at[0])
     head_halo.wait_recv()
     after = jnp.concatenate([halo[3]] * (LANES // SUBLANES), axis=0).T
     after = jnp.where(me < ctx - 1, after, 0.0)
@@ -398,29 +417,75 @@
             total = total + pltpu.roll(window, tok + LANES - j, 1)[:, :tok] * tap(j, rows)
         gk_ref[rows, :] = total
 
-    for (off, c), copy in cv_copies.items():
+    store(gk_ref, gk_hbm, store_sems.at[1])
+
+    for copy in (*cv_copies.values(), *cross_copies.values()):
         copy.wait_recv()
-    gq_ref[...] = go_ref[...] * cv_back[...]
-
-    for copy in cross_copies.values():
-        copy.wait_recv()
-    for z in range(ctx):
-        total = cross[z]
-        for off in range(1, seqs):
-            total = total + cross_in[off - 1, z]
-        gl_ref[:, z * tok : (z + 1) * tok] = total
+    for copy in stores:
+        copy.wait()
     for copy in started:
         copy.wait_send()
 
 
-def store(*refs):
-    count = (len(refs) - 1) // 2
-    copies = [
-        pltpu.make_async_copy(refs[i], refs[count + i], refs[-1].at[i]) for i in range(count)
+def finish(
+    gk_hbm,
+    gv_hbm,
+    go_hbm,
+    cv_hbm,
+    part_hbm,
+    cross_hbm,
+    gq_out,
+    gk_out,
+    gv_out,
+    gl_out,
+    gk_ref,
+    gv_ref,
+    go_ref,
+    cv_ref,
+    part_ref,
+    cross_ref,
+    gl_ref,
+    load_sems,
+    store_sems,
+):
+    pairs = (
+        (gk_hbm, gk_ref),
+        (gv_hbm, gv_ref),
+        (go_hbm, go_ref),
+        (cv_hbm, cv_ref),
+        (part_hbm, part_ref),
+        (cross_hbm, cross_ref),
+    )
+    loads = [
+        pltpu.make_async_copy(src, dst, load_sems.at[i]) for i, (src, dst) in enumerate(pairs)
     ]
-    for copy in copies:
+    for load in loads:
+        load.start()
+    stores = []
+
+    def store(src, dst):
+        copy = pltpu.make_async_copy(src, dst, store_sems.at[len(stores)])
         copy.start()
-    for copy in copies:
+        stores.append(copy)
+
+    loads[0].wait()
+    store(gk_ref, gk_out)
+    loads[1].wait()
+    store(gv_ref, gv_out)
+    loads[2].wait()
+    loads[3].wait()
+    cv_ref[...] = cv_ref[...] * go_ref[...]
+    store(cv_ref, gq_out)
+    loads[4].wait()
+    loads[5].wait()
+    ctx, _, tok = part_ref.shape
+    for z in range(ctx):
+        total = part_ref[z]
+        for other in range(cross_ref.shape[0]):
+            total = total + cross_ref[other, z]
+        gl_ref[:, z * tok : (z + 1) * tok] = total
+    store(gl_ref, gl_out)
+    for copy in stores:
         copy.wait()
 
 
@@ -435,7 +500,6 @@
     tables = make_tables(length)
     f32 = jnp.float32
     tokens = jax.ShapeDtypeStruct((chans, tok), f32)
-    vmem = pl.BlockSpec(memory_space=pltpu.VMEM)
     position = pltpu.VMEM((chans, tok), f32)
     channel = pltpu.VMEM((ctx, own, tok), f32)
     spectrum = pltpu.VMEM((bins, own, 2 * inner), f32)
@@ -445,10 +509,18 @@
     hbm = pl.BlockSpec(memory_space=pltpu.HBM)
     outs = pl.pallas_call(
         functools.partial(kernel, ctx, seqs),
-        out_shape=(tokens, tokens, tokens, jax.ShapeDtypeStruct((own, length), f32)),
+        out_shape=(
+            tokens,
+            tokens,
+            tokens,
+            jax.ShapeDtypeStruct((ctx, own, tok), f32),
+            jax.ShapeDtypeStruct((max(seqs - 1, 1), ctx, own, tok), f32),
+        ),
         in_specs=[hbm] * len(operands),
-        out_specs=(vmem,) * 4,
+        out_specs=(hbm,) * 5,
         scratch_shapes=[
+            position,
+            position,
             *(pltpu.VMEM(operands[i].shape, operands[i].dtype) for i in range(len(operands))),
             dma((len(operands),)),
             pltpu.VMEM((4, 2 * inner, 2 * inner), jnp.bfloat16),
@@ -462,9 +534,7 @@
             channel,
             channel,
             position,
-            position,
             channel,
-            pltpu.VMEM((max(seqs - 1, 1), ctx, own, tok), f32),
             spectrum,
             spectrum,
             spectrum,
@@ -476,19 +546,29 @@
             dma((seqs, chunks)),
             dma((2,)),
             dma((2,)),
+            dma((2,)),
+            dma((2, chunks)),
         ],
         compiler_params=pltpu.CompilerParams(
             collective_id=0, has_side_effects=True, vmem_limit_bytes=VMEM_BYTES
         ),
     )(*operands)
+    gk, gv, cv, part, cross = outs
+    operands = [gk, gv, operands[0], cv, part, cross]
+    result = jax.ShapeDtypeStruct((own, length), f32)
     gq, gk, gv, gl = pl.pallas_call(
-        store,
-        out_shape=tuple(jax.ShapeDtypeStruct(x.shape, f32) for x in outs),
-        in_specs=[hbm] * 4,
+        finish,
+        out_shape=(tokens, tokens, tokens, result),
+        in_specs=[hbm] * len(operands),
         out_specs=(hbm,) * 4,
-        scratch_shapes=[dma((4,))],
+        scratch_shapes=[
+            *(pltpu.VMEM(x.shape, f32) for x in operands),
+            pltpu.VMEM(result.shape, f32),
+            dma((len(operands),)),
+            dma((4,)),
+        ],
         compiler_params=pltpu.CompilerParams(vmem_limit_bytes=VMEM_BYTES),
-    )(*outs)
+    )(*operands)
     return (gq[None], gk[None], gv[None], gl)
 
 

time: 64.3 us -> 32.8 us (0.51)
  Pallas kernels: 63.5 us -> 32 us
    pallas_call x1, Pallas kernels: 32.9 us -> 2.16 us  [shards(): pl.pallas_call(finish, out_shape=(tokens, tokens, tokens, result), in_spe...]
    pallas_call x1, Pallas kernels: 30.6 us -> 29.9 us  [shards(): pl.pallas_call(functools.partial(kernel, ctx, seqs), out_shape=(tokens, t...]
where the time goes in v2:
time: 32.8 us; the launch traced here: 32.7 us
  Pallas kernels  32 us (98%)
  between operations  0.64 us (2%)
    pallas_call x1, Pallas kernels, shards(): pl.pallas_call(functools.partial(kernel, ctx, seqs), out_shape=(tokens, t...  29.9 us
    pallas_call x1, Pallas kernels, shards(): pl.pallas_call(finish, out_shape=(tokens, tokens, tokens, result), in_spe...  2.16 us

profile of v2, /device:TPU:0, one launch (start us, length us, event | category | flops | bytes accessed | tf_op | source)
XLA Modules:
  0.0 32.7 jit_solution(17375264078765833620)
XLA Ops:
  0.6 29.9 %shard_map.111 = (f32[128,512]{1,0:T(8,128)}, f32[128,512]{1,0:T(8,128)}, f32[128,512]{1,0:T(8,128)}, f32[4,32,512]{2,1,0:T(8,128)}, f32[1,4,32,512]{3,2,1,0:T(8,128)}) custom-call(f32[128,512]{1,0:T(8,128)} %bitcast.8, f32[128,512]{1,0:T(8,128)} %bitcast.10, f32[128,512]{1,0:T(8,128)} %bitcast.11, f32[128,512]{1,0:T(8,128)} %bitcast.12, f32[32,2048]{1,0:T(8,128)} %lf_hbm.1, ...), custom_call_target="tpu_custom_call" | custom-call | tf_op jit(solution)/shard_map/pallas_call | solution.py:510
  30.5 2.2 %shard_map.112 = (f32[128,512]{1,0:T(8,128)}, f32[128,512]{1,0:T(8,128)}, f32[128,512]{1,0:T(8,128)}, f32[32,2048]{1,0:T(8,128)}) custom-call(f32[128,512]{1,0:T(8,128)} %get-tuple-element.13.gk_hbm, f32[128,512]{1,0:T(8,128)} %get-tuple-element.14.gv_hbm, f32[128,512]{1,0:T(8,128)} %bitcast.9, f32[128,512]{1,0:T(8,128)} %get-tuple-element.15.cv_hbm, ...), custom_call_target="tpu_custom_call" | custom-call | tf_op jit(solution)/shard_map/pallas_call | solution.py:559

commit v3 on v2

--- a/solution.py
+++ b/solution.py
@@ -495,7 +495,7 @@
     length = tok * ctx
     _, outer, inner = plan(length)
     bins = outer // 2 + 1
-    chunk = math.gcd(own, 16)
+    chunk = math.gcd(own, 8)
     chunks = own // chunk
     tables = make_tables(length)
     f32 = jnp.float32

time: 32.8 us -> 33.6 us (1.024)
  Pallas kernels: 32 us -> 32.8 us
    pallas_call x1, Pallas kernels: 29.9 us -> 30.6 us  [shards(): pl.pallas_call(functools.partial(kernel, ctx, seqs), out_shape=(tokens, t...]
where the time goes in v3:
time: 33.6 us; the launch traced here: 33.4 us
  Pallas kernels  32.8 us (98%)
  between operations  0.64 us (2%)
    pallas_call x1, Pallas kernels, shards(): pl.pallas_call(functools.partial(kernel, ctx, seqs), out_shape=(tokens, t...  30.6 us
    pallas_call x1, Pallas kernels, shards(): pl.pallas_call(finish, out_shape=(tokens, tokens, tokens, result), in_spe...  2.16 us

profile of v3, /device:TPU:0, one launch (start us, length us, event | category | flops | bytes accessed | tf_op | source)
XLA Modules:
  0.0 33.4 jit_solution(1737587418853475880)
XLA Ops:
  0.6 30.6 %shard_map.111 = (f32[128,512]{1,0:T(8,128)}, f32[128,512]{1,0:T(8,128)}, f32[128,512]{1,0:T(8,128)}, f32[4,32,512]{2,1,0:T(8,128)}, f32[1,4,32,512]{3,2,1,0:T(8,128)}) custom-call(f32[128,512]{1,0:T(8,128)} %bitcast.8, f32[128,512]{1,0:T(8,128)} %bitcast.10, f32[128,512]{1,0:T(8,128)} %bitcast.11, f32[128,512]{1,0:T(8,128)} %bitcast.12, f32[32,2048]{1,0:T(8,128)} %lf_hbm.1, ...), custom_call_target="tpu_custom_call" | custom-call | tf_op jit(solution)/shard_map/pallas_call | solution.py:510
  31.2 2.2 %shard_map.112 = (f32[128,512]{1,0:T(8,128)}, f32[128,512]{1,0:T(8,128)}, f32[128,512]{1,0:T(8,128)}, f32[32,2048]{1,0:T(8,128)}) custom-call(f32[128,512]{1,0:T(8,128)} %get-tuple-element.13.gk_hbm, f32[128,512]{1,0:T(8,128)} %get-tuple-element.14.gv_hbm, f32[128,512]{1,0:T(8,128)} %bitcast.9, f32[128,512]{1,0:T(8,128)} %get-tuple-element.15.cv_hbm, ...), custom_call_target="tpu_custom_call" | custom-call | tf_op jit(solution)/shard_map/pallas_call | solution.py:559

commit v4 on v2

--- a/solution.py
+++ b/solution.py
@@ -189,6 +189,8 @@
         )
 
     def block(start, size):
+        if isinstance(start, int):
+            return pl.ds(start, size)
         return pl.ds(pl.multiple_of(start, SUBLANES), size)
 
     def out_copy(kind, src, dst, off, c):
@@ -264,18 +266,14 @@
         high = x.astype(jnp.bfloat16)
         return high, (x - high.astype(jnp.float32)).astype(jnp.bfloat16)
 
-    def table(i):
-        return table_split[i]
-
-    def multiply(first):
-        x = work[...].reshape(bins * chunk, 2 * inner)
-        high, low = split(x)
-        dot = functools.partial(jnp.dot, preferred_element_type=jnp.float32)
-        y = dot(high, table(first)) + dot(low, table(first)) + dot(high, table(first + 1))
+    def multiply(x, which):
+        high, low = split(x.reshape(bins * chunk, 2 * inner))
+        parts = jnp.concatenate([high, low, high], axis=1)
+        y = jnp.dot(parts, table_split[which], preferred_element_type=jnp.float32)
         return y.reshape(bins, chunk, 2 * inner)
 
     def transform(load, c, spec):
-        def rows_step(i, carry):
+        def rows_step(i):
             base = c * chunk + i * SUBLANES
             for lane in range(0, inner, LANES):
                 x = [load(t, base, lane) for t in range(outer // 2)]
@@ -292,10 +290,10 @@
                     at = block(i * SUBLANES, SUBLANES)
                     work[k, at, lane : lane + LANES] = re
                     work[k, at, inner + lane : inner + lane + LANES] = im
-            return carry
-
-        lax.fori_loop(0, chunk // SUBLANES, rows_step, 0)
-        spec[:, c * chunk : (c + 1) * chunk, :] = multiply(0)
+
+        for i in range(chunk // SUBLANES):
+            rows_step(i)
+        spec[:, c * chunk : (c + 1) * chunk, :] = multiply(work[...], 0)
 
     def load_from(ref):
         def load(t, base, lane):
@@ -311,23 +309,18 @@
     def product(a, b, c, conjugate):
         rows = slice(c * chunk, (c + 1) * chunk)
 
-        def step(k, carry):
-            ar, ai = a[k, rows, :inner], a[k, rows, inner:]
-            br, bi = b[k, rows, :inner], b[k, rows, inner:]
-            if conjugate:
-                work[k, :, :inner] = ar * br + ai * bi
-                work[k, :, inner:] = ai * br - ar * bi
-            else:
-                work[k, :, :inner] = ar * br - ai * bi
-                work[k, :, inner:] = ar * bi + ai * br
-            return carry
-
-        lax.fori_loop(0, bins, step, 0)
-
-    def inverse(c, dst):
-        work[...] = multiply(2)
-
-        def rows_step(i, carry):
+        ar, ai = a[:, rows, :inner], a[:, rows, inner:]
+        br, bi = b[:, rows, :inner], b[:, rows, inner:]
+        if conjugate:
+            re, im = ar * br + ai * bi, ai * br - ar * bi
+        else:
+            re, im = ar * br - ai * bi, ar * bi + ai * br
+        return jnp.concatenate([re, im], axis=2)
+
+    def inverse(x, c, dst):
+        work[...] = multiply(x, 1)
+
+        def rows_step(i):
             at = block(i * SUBLANES, SUBLANES)
             for lane in range(0, inner, LANES):
                 z = []
@@ -343,9 +336,9 @@
                 for t, x in enumerate(half_ifft(z)):
                     col = (t % per_tok) * inner + lane
                     dst[t // per_tok, block(c * chunk + i * SUBLANES, SUBLANES), col : col + LANES] = x
-            return carry
-
-        lax.fori_loop(0, chunk // SUBLANES, rows_step, 0)
+
+        for i in range(chunk // SUBLANES):
+            rows_step(i)
 
     def own_rows(c):
         return block(me * own + c * chunk, chunk)
@@ -365,7 +358,9 @@
     table_load.wait()
     for i in range(2):
         whole = table_ref[i * 2 * inner : (i + 1) * 2 * inner, :]
-        table_split[2 * i], table_split[2 * i + 1] = split(whole)
+        high, low = split(whole)
+        for part, value in enumerate((high, high, low)):
+            table_split[i, part * 2 * inner : (part + 1) * 2 * inner, :] = value
     for c in range(chunks):
         transform(load_filter, c, spec_h)
 
@@ -374,8 +369,7 @@
         for off in range(1, ctx):
             d_copies[off, c].wait_recv()
         transform(load_from(d_own), c, spec_d)
-        product(spec_d, spec_h, c, True)
-        inverse(c, gg_src)
+        inverse(product(spec_d, spec_h, c, True), c, gg_src)
         for off in range(ctx - 1, 0, -1):
             gg_copies[off, c] = start(back_copy(2, gg_src, gg_back, off, c))
         gg_back[own_rows(c)] = gg_src[me, chunk_rows(c)]
@@ -383,12 +377,10 @@
         for off in range(1, ctx):
             g_copies[off, c].wait_recv()
         transform(load_from(g_own), c, spec_g)
-        product(spec_g, spec_h, c, False)
-        inverse(c, cv_src)
+        inverse(product(spec_g, spec_h, c, False), c, cv_src)
         for off in range(ctx - 1, 0, -1):
             cv_copies[off, c] = start(back_copy(3, cv_src, cv_back, off, c))
-        product(spec_d, spec_g, c, True)
-        inverse(c, cross)
+        inverse(product(spec_d, spec_g, c, True), c, cross)
         for off in range(1, seqs):
             cross_copies[off, c] = start(cross_copy(off, c))
         store(cv_src.at[me, chunk_rows(c)], cv_back.at[own_rows(c)], keep_sems.at[0, c])
@@ -523,7 +515,7 @@
             position,
             *(pltpu.VMEM(operands[i].shape, operands[i].dtype) for i in range(len(operands))),
             dma((len(operands),)),
-            pltpu.VMEM((4, 2 * inner, 2 * inner), jnp.bfloat16),
+            pltpu.VMEM((2, 6 * inner, 2 * inner), jnp.bfloat16),
             pltpu.VMEM((short_filter.shape[1], chans, LANES), f32),
             position,
             position,

time: 32.8 us -> 32.8 us (level)
  no operation moved by 1% of the time
where the time goes in v4:
time: 32.8 us; the launch traced here: 32.6 us
  Pallas kernels  32 us (98%)
  between operations  0.64 us (2%)
    pallas_call x1, Pallas kernels, shards(): pl.pallas_call(functools.partial(kernel, ctx, seqs), out_shape=(tokens, t...  29.8 us
    pallas_call x1, Pallas kernels, shards(): pl.pallas_call(finish, out_shape=(tokens, tokens, tokens, result), in_spe...  2.16 us

profile of v4, /device:TPU:0, one launch (start us, length us, event | category | flops | bytes accessed | tf_op | source)
XLA Modules:
  0.0 32.6 jit_solution(13288847326743842884)
XLA Ops:
  0.6 29.8 %shard_map.111 = (f32[128,512]{1,0:T(8,128)}, f32[128,512]{1,0:T(8,128)}, f32[128,512]{1,0:T(8,128)}, f32[4,32,512]{2,1,0:T(8,128)}, f32[1,4,32,512]{3,2,1,0:T(8,128)}) custom-call(f32[128,512]{1,0:T(8,128)} %bitcast.8, f32[128,512]{1,0:T(8,128)} %bitcast.10, f32[128,512]{1,0:T(8,128)} %bitcast.11, f32[128,512]{1,0:T(8,128)} %bitcast.12, f32[32,2048]{1,0:T(8,128)} %lf_hbm.1, ...), custom_call_target="tpu_custom_call" | custom-call | tf_op jit(solution)/shard_map/pallas_call | solution.py:502
  30.5 2.2 %shard_map.112 = (f32[128,512]{1,0:T(8,128)}, f32[128,512]{1,0:T(8,128)}, f32[128,512]{1,0:T(8,128)}, f32[32,2048]{1,0:T(8,128)}) custom-call(f32[128,512]{1,0:T(8,128)} %get-tuple-element.13.gk_hbm, f32[128,512]{1,0:T(8,128)} %get-tuple-element.14.gv_hbm, f32[128,512]{1,0:T(8,128)} %bitcast.9, f32[128,512]{1,0:T(8,128)} %get-tuple-element.15.cv_hbm, ...), custom_call_target="tpu_custom_call" | custom-call | tf_op jit(solution)/shard_map/pallas_call | solution.py:551

commit v5 on v4

--- a/solution.py
+++ b/solution.py
@@ -487,7 +487,7 @@
     length = tok * ctx
     _, outer, inner = plan(length)
     bins = outer // 2 + 1
-    chunk = math.gcd(own, 16)
+    chunk = math.gcd(own, 32)
     chunks = own // chunk
     tables = make_tables(length)
     f32 = jnp.float32

time: 32.8 us -> 32.2 us (0.982)
  Pallas kernels: 32 us -> 31.4 us
    pallas_call x1, Pallas kernels: 29.8 us -> 29.3 us  [shards(): pl.pallas_call(functools.partial(kernel, ctx, seqs), out_shape=(tokens, t...]
where the time goes in v5:
time: 32.2 us; the launch traced here: 32.1 us
  Pallas kernels  31.4 us (98%)
  between operations  0.64 us (2%)
    pallas_call x1, Pallas kernels, shards(): pl.pallas_call(functools.partial(kernel, ctx, seqs), out_shape=(tokens, t...  29.3 us
    pallas_call x1, Pallas kernels, shards(): pl.pallas_call(finish, out_shape=(tokens, tokens, tokens, result), in_spe...  2.16 us

profile of v5, /device:TPU:0, one launch (start us, length us, event | category | flops | bytes accessed | tf_op | source)
XLA Modules:
  0.0 32.1 jit_solution(643428756167689953)
XLA Ops:
  0.6 29.3 %shard_map.111 = (f32[128,512]{1,0:T(8,128)}, f32[128,512]{1,0:T(8,128)}, f32[128,512]{1,0:T(8,128)}, f32[4,32,512]{2,1,0:T(8,128)}, f32[1,4,32,512]{3,2,1,0:T(8,128)}) custom-call(f32[128,512]{1,0:T(8,128)} %bitcast.8, f32[128,512]{1,0:T(8,128)} %bitcast.10, f32[128,512]{1,0:T(8,128)} %bitcast.11, f32[128,512]{1,0:T(8,128)} %bitcast.12, f32[32,2048]{1,0:T(8,128)} %lf_hbm.1, ...), custom_call_target="tpu_custom_call" | custom-call | tf_op jit(solution)/shard_map/pallas_call | solution.py:502
  29.9 2.2 %shard_map.112 = (f32[128,512]{1,0:T(8,128)}, f32[128,512]{1,0:T(8,128)}, f32[128,512]{1,0:T(8,128)}, f32[32,2048]{1,0:T(8,128)}) custom-call(f32[128,512]{1,0:T(8,128)} %get-tuple-element.13.gk_hbm, f32[128,512]{1,0:T(8,128)} %get-tuple-element.14.gv_hbm, f32[128,512]{1,0:T(8,128)} %bitcast.9, f32[128,512]{1,0:T(8,128)} %get-tuple-element.15.cv_hbm, ...), custom_call_target="tpu_custom_call" | custom-call | tf_op jit(solution)/shard_map/pallas_call | solution.py:551

commit v6 on v5

--- a/solution.py
+++ b/solution.py
@@ -370,11 +370,12 @@
             d_copies[off, c].wait_recv()
         transform(load_from(d_own), c, spec_d)
         inverse(product(spec_d, spec_h, c, True), c, gg_src)
-        for off in range(ctx - 1, 0, -1):
-            gg_copies[off, c] = start(back_copy(2, gg_src, gg_back, off, c))
         gg_back[own_rows(c)] = gg_src[me, chunk_rows(c)]
     for c in range(chunks):
         for off in range(1, ctx):
+            if off == ctx - 1:
+                for back in range(ctx - 1, 0, -1):
+                    gg_copies[back, c] = start(back_copy(2, gg_src, gg_back, back, c))
             g_copies[off, c].wait_recv()
         transform(load_from(g_own), c, spec_g)
         inverse(product(spec_g, spec_h, c, False), c, cv_src)

time: 32.2 us -> 33.3 us (1.034)
  Pallas kernels: 31.4 us -> 32.5 us
    pallas_call x1, Pallas kernels: 29.3 us -> 30.4 us  [shards(): pl.pallas_call(functools.partial(kernel, ctx, seqs), out_shape=(tokens, t...]
where the time goes in v6:
time: 33.3 us; the launch traced here: 33.2 us
  Pallas kernels  32.5 us (98%)
  between operations  0.64 us (2%)
    pallas_call x1, Pallas kernels, shards(): pl.pallas_call(functools.partial(kernel, ctx, seqs), out_shape=(tokens, t...  30.4 us
    pallas_call x1, Pallas kernels, shards(): pl.pallas_call(finish, out_shape=(tokens, tokens, tokens, result), in_spe...  2.16 us

profile of v6, /device:TPU:0, one launch (start us, length us, event | category | flops | bytes accessed | tf_op | source)
XLA Modules:
  0.0 33.2 jit_solution(11226141299139956853)
XLA Ops:
  0.6 30.4 %shard_map.111 = (f32[128,512]{1,0:T(8,128)}, f32[128,512]{1,0:T(8,128)}, f32[128,512]{1,0:T(8,128)}, f32[4,32,512]{2,1,0:T(8,128)}, f32[1,4,32,512]{3,2,1,0:T(8,128)}) custom-call(f32[128,512]{1,0:T(8,128)} %bitcast.8, f32[128,512]{1,0:T(8,128)} %bitcast.10, f32[128,512]{1,0:T(8,128)} %bitcast.11, f32[128,512]{1,0:T(8,128)} %bitcast.12, f32[32,2048]{1,0:T(8,128)} %lf_hbm.1, ...), custom_call_target="tpu_custom_call" | custom-call | tf_op jit(solution)/shard_map/pallas_call | solution.py:503
  31.0 2.2 %shard_map.112 = (f32[128,512]{1,0:T(8,128)}, f32[128,512]{1,0:T(8,128)}, f32[128,512]{1,0:T(8,128)}, f32[32,2048]{1,0:T(8,128)}) custom-call(f32[128,512]{1,0:T(8,128)} %get-tuple-element.13.gk_hbm, f32[128,512]{1,0:T(8,128)} %get-tuple-element.14.gv_hbm, f32[128,512]{1,0:T(8,128)} %bitcast.9, f32[128,512]{1,0:T(8,128)} %get-tuple-element.15.cv_hbm, ...), custom_call_target="tpu_custom_call" | custom-call | tf_op jit(solution)/shard_map/pallas_call | solution.py:552
